TPU v7x, 128 devices: a whole 4x4x4 slice. The times are simulated.
128 devices in a mesh: seq: 4 (over x), ep: 32 (over z, y, core).
Axes of the slice: x: 4, y: 4, z: 4, core: 2. Of those that a mesh axis runs over, the one named last changes fastest.
Arguments:
- tokens: bfloat16 [1024, 7168], P(('seq', 'ep')), may hold values from -50 to 50
- out_grad: bfloat16 [1024, 7168], P(('seq', 'ep')), may hold values from -24 to 24
- routes: int32 [1024, 8], P(('seq', 'ep')), may hold values from 0 to 31, all different within a row; in each aligned block of 8 rows (0 to 7, 8 to 15, ...) at most 2 rows name the same one
- gate_fixed: int32 [1024, 8], P(('seq', 'ep')), may hold values from 1 to 65535
- ramp_step: int32 [32], replicated, may hold values from 1 to 8
- norm_gain: float32 [7168], replicated, may hold values from 0.1 to 1.9
- w_gate: bfloat16 [32, 7168, 1024], P('ep', None, 'seq'), may hold values from -0.0625 to 0.0625
- w_up: bfloat16 [32, 7168, 1024], P('ep', None, 'seq'), may hold values from -0.0625 to 0.0625
- w_down: bfloat16 [32, 1024, 7168], P('ep', 'seq'), may hold values from -0.1875 to 0.1875
Outputs:
- mixed: bfloat16 [1024, 7168], P(('seq', 'ep'))
- tokens_grad: bfloat16 [1024, 7168], P(('seq', 'ep'))
- gain_grad: float32 [7168], P(('seq', 'ep'))
- w_gate_grad: bfloat16 [32, 7168, 1024], P('ep', None, 'seq')
- w_up_grad: bfloat16 [32, 7168, 1024], P('ep', None, 'seq')
- w_down_grad: bfloat16 [32, 1024, 7168], P('ep', 'seq')
Inputs may be any that keep to these rules, and one draw needn't show every extreme that they name: `routes`: each row names 8 different experts. Within the rows of one device (aligned blocks of 8 rows) no expert is named more than 2 times, and in some such block one expert is named exactly 2 times.
All inputs are finite; a program needn't handle non-finite values.
Results may differ from a plain program's by a relative error of at most 0.023.
Values may be sent and summed in bfloat16 or wider, within the bound.
A program may use at most 128 MiB of HBM per device.

v0:
```python
import jax
import jax.numpy as jnp
from jax import lax
from jax.sharding import PartitionSpec as P

RAMP = 8


gate_unit = 65536.0
norm_eps = 1e-06


def contract_rows(left, right):
    return lax.dot_general(
        left, right, (((0,), (0,)), ((), ())), preferred_element_type=jnp.float32
    )


def contract_cols(left, right):
    return lax.dot_general(
        left, right, (((1,), (1,)), ((), ())), preferred_element_type=jnp.float32
    )


def dispatch(send_normed, send_grad, seq_count, experts, capacity):
    width = send_normed.shape[1]

    def spread(buffer):
        wide = jnp.broadcast_to(
            buffer.reshape(1, experts, capacity, width), (seq_count, experts, capacity, width)
        )
        return wide.reshape(seq_count * experts, capacity, width)

    got_normed, got_grad = (
        lax.all_to_all(spread(send_normed), ("seq", "ep"), split_axis=0, concat_axis=0, tiled=True),
        lax.all_to_all(spread(send_grad), ("seq", "ep"), split_axis=0, concat_axis=0, tiled=True),
    )
    return (got_normed.reshape(-1, width), got_grad.reshape(-1, width))


def collect(out_part, back_part, seq_count, ep_count, capacity):
    width = out_part.shape[1]

    def shaped(values):
        return values.astype(jnp.bfloat16).reshape(seq_count * ep_count, capacity, width)

    def folded(values):
        wide = values.astype(jnp.float32).reshape(seq_count, ep_count * capacity, width)
        return jnp.sum(wide, axis=0).astype(jnp.bfloat16)

    got_out, got_back = (
        lax.all_to_all(shaped(out_part), ("seq", "ep"), split_axis=0, concat_axis=0, tiled=True),
        lax.all_to_all(shaped(back_part), ("seq", "ep"), split_axis=0, concat_axis=0, tiled=True),
    )
    return (folded(got_out), folded(got_back))


def on_device(tokens, out_grad, routes, gate_fixed, ramp_step, norm_gain, w_gate, w_up, w_down):
    seq_count = lax.axis_size("seq")
    ep_count = lax.axis_size("ep")
    rows_dev, width = tokens.shape
    top_count = routes.shape[1]
    capacity = min(rows_dev, 5 * rows_dev * top_count // (4 * ep_count))
    tokens_wide = tokens.astype(jnp.float32)
    recip = lax.rsqrt(jnp.mean(tokens_wide * tokens_wide, axis=1, keepdims=True) + norm_eps)
    normed = (tokens_wide * recip * norm_gain[None, :]).astype(jnp.bfloat16)
    flat_routes = routes.reshape(-1)
    onehot = (flat_routes[:, None] == jnp.arange(ep_count, dtype=jnp.int32)[None, :]).astype(
        jnp.int32
    )
    position = jnp.sum(jnp.cumsum(onehot, axis=0) * onehot, axis=1) - 1
    slot_index = flat_routes * capacity + position
    ramp_pick = jnp.sum(onehot * ramp_step[None, :], axis=1).astype(jnp.float32)
    coef = gate_fixed.reshape(-1).astype(jnp.float32) / gate_unit * ramp_pick / RAMP
    grad_rows = (
        coef[:, None] * jnp.repeat(out_grad.astype(jnp.float32), top_count, axis=0)
    ).astype(jnp.bfloat16)
    normed_rows = jnp.repeat(normed, top_count, axis=0)
    empty = jnp.zeros((ep_count * capacity, width), jnp.bfloat16)
    send_normed = empty.at[slot_index].set(normed_rows)
    send_grad = empty.at[slot_index].set(grad_rows)
    in_normed, in_grad = dispatch(send_normed, send_grad, seq_count, ep_count, capacity)
    weight_gate = w_gate[0]
    weight_up = w_up[0]
    weight_down = w_down[0]
    pre_gate = jnp.dot(in_normed, weight_gate, preferred_element_type=jnp.float32)
    pre_up = jnp.dot(in_normed, weight_up, preferred_element_type=jnp.float32)
    sigma = jax.nn.sigmoid(pre_gate)
    active = pre_gate * sigma
    hidden = (active * pre_up).astype(jnp.bfloat16)
    out_part = jnp.dot(hidden, weight_down, preferred_element_type=jnp.float32)
    hidden_grad = contract_cols(in_grad, weight_down)
    gate_pre_grad = (hidden_grad * pre_up * sigma * (1.0 + pre_gate * (1.0 - sigma))).astype(
        jnp.bfloat16
    )
    up_pre_grad = (hidden_grad * active).astype(jnp.bfloat16)
    w_down_grad = contract_rows(hidden, in_grad).astype(jnp.bfloat16)[None]
    w_gate_grad = contract_rows(in_normed, gate_pre_grad).astype(jnp.bfloat16)[None]
    w_up_grad = contract_rows(in_normed, up_pre_grad).astype(jnp.bfloat16)[None]
    back_part = contract_cols(gate_pre_grad, weight_gate) + contract_cols(up_pre_grad, weight_up)
    slot_out, slot_back = collect(out_part, back_part, seq_count, ep_count, capacity)
    picked_out = slot_out[slot_index].astype(jnp.float32).reshape(rows_dev, top_count, width)
    picked_back = slot_back[slot_index].astype(jnp.float32).reshape(rows_dev, top_count, width)
    mixed = jnp.sum(coef.reshape(rows_dev, top_count, 1) * picked_out, axis=1).astype(jnp.bfloat16)
    normed_grad = jnp.sum(picked_back, axis=1)
    gain_term = jnp.sum(normed_grad * tokens_wide * recip, axis=0)
    gain_grad = lax.psum_scatter(gain_term, ("seq", "ep"), scatter_dimension=0, tiled=True)
    scaled = norm_gain[None, :] * normed_grad
    inner = jnp.sum(scaled * tokens_wide, axis=1, keepdims=True)
    tokens_grad = (recip * scaled - tokens_wide * recip * recip * recip * inner / width).astype(
        jnp.bfloat16
    )
    return (mixed, tokens_grad, gain_grad, w_gate_grad, w_up_grad, w_down_grad)


def solution(mesh):
    return jax.shard_map(
        on_device,
        mesh=mesh,
        in_specs=(
            P(("seq", "ep"), None),
            P(("seq", "ep"), None),
            P(("seq", "ep"), None),
            P(("seq", "ep"), None),
            P(),
            P(),
            P("ep", None, "seq"),
            P("ep", None, "seq"),
            P("ep", "seq", None),
        ),
        out_specs=(
            P(("seq", "ep"), None),
            P(("seq", "ep"), None),
            P(("seq", "ep")),
            P("ep", None, "seq"),
            P("ep", None, "seq"),
            P("ep", "seq", None),
        ),
        check_vma=False,
    )
```

profile of v0, /device:TPU:1, one launch (start us, length us, event | category | flops | bytes accessed | tf_op | source)
XLA Modules:
  0.0 326.0 jit_solution(2742865277095432240)
XLA Ops:
  7.7 3.7 %broadcast_in_dim.46 = bf16[4,32,2,7168]{3,2,1,0:T(2,128)(2,1)} broadcast(bf16[32,2,7168]{2,1,0:T(2,128)(2,1)S(1)} %broadcast_in_dim.22), dimensions={1,2,3} | broadcast | bytes 4587520 | tf_op jit(solution)/shard_map/broadcast_in_dim | solution.py:29
  11.4 11.9 %all-to-all-start = ((bf16[128,2,7168]{2,1,0:T(2,128)(2,1)}), bf16[128,2,7168]{2,1,0:T(2,128)(2,1)}, u32[]{:S(2)}, u32[]{:S(2)}) async-start(bf16[128,2,7168]{2,1,0:T(2,128)(2,1)} %bitcast.57), calls=%async_computation | async-start | bytes 7340032 | tf_op jit(solution)/shard_map/all_to_all | solution.py:35
  26.1 44.3 %all-to-all-done = bf16[128,2,7168]{2,1,0:T(2,128)(2,1)} async-done(((bf16[128,2,7168]{2,1,0:T(2,128)(2,1)}), bf16[128,2,7168]{2,1,0:T(2,128)(2,1)}, u32[]{:S(2)}, u32[]{:S(2)}) %all-to-all-start) | async-done | bytes 3670048 | tf_op jit(solution)/shard_map/all_to_all | solution.py:35
  70.3 3.7 %broadcast_in_dim.49 = bf16[4,32,2,7168]{3,2,1,0:T(2,128)(2,1)} broadcast(bf16[32,2,7168]{2,1,0:T(2,128)(2,1)S(1)} %broadcast_in_dim.48), dimensions={1,2,3} | broadcast | bytes 4587520 | tf_op jit(solution)/shard_map/broadcast_in_dim | solution.py:29
  74.0 5.7 %all-to-all-start.2 = ((bf16[128,2,7168]{2,1,0:T(2,128)(2,1)}), bf16[128,2,7168]{2,1,0:T(2,128)(2,1)}, u32[]{:S(2)}, u32[]{:S(2)}) async-start(bf16[128,2,7168]{2,1,0:T(2,128)(2,1)} %bitcast.58), calls=%async_computation.2 | async-start | bytes 7340032 | tf_op jit(solution)/shard_map/all_to_all | solution.py:36
  79.7 8.4 %reshape.134 = bf16[256,7168]{1,0:T(8,128)(2,1)} reshape(bf16[128,2,7168]{2,1,0:T(2,128)(2,1)} %all-to-all-done) | data formatting | bytes 7340032 | tf_op jit(solution)/shard_map/reshape | solution.py:38
  88.1 4.4 %fusion.12 = f32[256,256]{1,0:T(8,128)S(1)} fusion(bf16[256,7168]{1,0:T(8,128)(2,1)} %reshape.134, bf16[1,7168,256]{2,1,0:T(8,128)(2,1)} %param.15), kind=kOutput, calls=%fused_computation.21 | convolution fusion | flops 939524096 | bytes 7602176 | tf_op jit(solution)/shard_map/dot_general | solution.py:86
  94.5 32.3 %all-to-all-done.2 = bf16[128,2,7168]{2,1,0:T(2,128)(2,1)} async-done(((bf16[128,2,7168]{2,1,0:T(2,128)(2,1)}), bf16[128,2,7168]{2,1,0:T(2,128)(2,1)}, u32[]{:S(2)}, u32[]{:S(2)}) %all-to-all-start.2) | async-done | bytes 3670048 | tf_op jit(solution)/shard_map/all_to_all | solution.py:36
  126.8 8.4 %reshape.140 = bf16[256,7168]{1,0:T(8,128)(2,1)} reshape(bf16[128,2,7168]{2,1,0:T(2,128)(2,1)} %all-to-all-done.2) | data formatting | bytes 7340032 | tf_op jit(solution)/shard_map/reshape | solution.py:38
  135.2 4.5 %multiply_convert_fusion = (bf16[256,256]{1,0:T(8,128)(2,1)S(1)}, bf16[256,256]{1,0:T(8,128)(2,1)S(1)}, bf16[256,256]{1,0:T(8,128)(2,1)S(1)}) fusion(f32[256,256]{1,0:T(8,128)S(1)} %fusion.12, f32[256,256]{1,0:T(8,128)S(1)} %fusion.8, bf16[256,7168]{1,0:T(8,128)(2,1)} %reshape.140, bf16[1,256,7168]{2,1,0:T(8,128)(2,1)} %param.17), kind=kOutput, calls=%fused_computation.42 | convolution fusion | flops 940507136 | bytes 8257536 | tf_op jit(solution)/shard_map/dot_general | solution.py:20
  141.7 3.0 fusion
  144.7 8.1 %reshape.141 = bf16[128,2,7168]{2,1,0:T(2,128)(2,1)} reshape(bf16[256,7168]{1,0:T(8,128)(2,1)} %fusion) | data formatting | bytes 7340032 | tf_op jit(solution)/shard_map/reshape | solution.py:45
  152.8 5.6 %all-to-all-start.3 = ((bf16[128,2,7168]{2,1,0:T(2,128)(2,1)}), bf16[128,2,7168]{2,1,0:T(2,128)(2,1)}, u32[]{:S(2)}, u32[]{:S(2)}) async-start(bf16[128,2,7168]{2,1,0:T(2,128)(2,1)} %reshape.141), calls=%async_computation.3 | async-start | bytes 7340032 | tf_op jit(solution)/shard_map/all_to_all | solution.py:53
  158.5 5.0 %convolution_convert_fusion.3 = bf16[256,7168]{1,0:T(8,128)(2,1)} fusion(bf16[256,256]{1,0:T(8,128)(2,1)S(1)} %get-tuple-element.12, bf16[1,256,7168]{2,1,0:T(8,128)(2,1)} %param.17), kind=kOutput, calls=%fused_computation.9 | convolution fusion | flops 941359104 | bytes 7471104 | tf_op jit(solution)/shard_map/dot_general | solution.py:91
  163.5 8.1 %reshape.135 = bf16[128,2,7168]{2,1,0:T(2,128)(2,1)} reshape(bf16[256,7168]{1,0:T(8,128)(2,1)} %convolution_convert_fusion.3) | data formatting | bytes 7340032 | tf_op jit(solution)/shard_map/reshape | solution.py:45
  171.6 34.0 %all-to-all-done.3 = bf16[128,2,7168]{2,1,0:T(2,128)(2,1)} async-done(((bf16[128,2,7168]{2,1,0:T(2,128)(2,1)}), bf16[128,2,7168]{2,1,0:T(2,128)(2,1)}, u32[]{:S(2)}, u32[]{:S(2)}) %all-to-all-start.3) | async-done | bytes 3670048 | tf_op jit(solution)/shard_map/all_to_all | solution.py:53
  205.6 5.9 %all-to-all-start.1 = ((bf16[128,2,7168]{2,1,0:T(2,128)(2,1)}), bf16[128,2,7168]{2,1,0:T(2,128)(2,1)}, u32[]{:S(2)}, u32[]{:S(2)}) async-start(bf16[128,2,7168]{2,1,0:T(2,128)(2,1)} %reshape.135), calls=%async_computation.1 | async-start | bytes 7340032 | tf_op jit(solution)/shard_map/all_to_all | solution.py:52
  211.5 5.2 %fusion.3 = bf16[1,256,7168]{2,1,0:T(8,128)(2,1)} fusion(bf16[256,256]{1,0:T(8,128)(2,1)S(1)} %get-tuple-element.12, bf16[256,7168]{1,0:T(8,128)(2,1)} %reshape.140), kind=kOutput, calls=%fused_computation.12 | convolution fusion | flops 941359104 | bytes 7471104 | tf_op jit(solution)/shard_map/dot_general | solution.py:14
  216.7 3.0 fusion.1
  219.7 3.0 fusion.2
  222.7 8.4 %reshape.142 = bf16[4,64,7168]{2,1,0:T(8,128)(2,1)} reshape(bf16[128,2,7168]{2,1,0:T(2,128)(2,1)} %all-to-all-done.3) | data formatting | bytes 7340032 | tf_op jit(solution)/shard_map/reshape | solution.py:48
  231.1 2.8 reduce.1
  235.9 75.0 %all-reduce = f32[7168]{0:T(1024)S(1)} all-reduce(f32[7168]{0:T(1024)S(1)} %get-tuple-element.6), channel_id=2, replica_groups=mesh['seq'=4,'ep'=32] {'seq','ep'}, use_global_device_ids=true, to_apply=%region_12.13.clone | all-reduce | flops 7168 | bytes 57344
  311.7 8.4 %reshape.136 = bf16[4,64,7168]{2,1,0:T(8,128)(2,1)} reshape(bf16[128,2,7168]{2,1,0:T(2,128)(2,1)} %all-to-all-done.1) | data formatting | bytes 7340032 | tf_op jit(solution)/shard_map/reshape | solution.py:48
  (50 shorter events, 22.4 us)
Async XLA Ops:
  11.4 12.0 %copy-start.8 = (s32[8,8]{1,0:T(8,128)S(1)}, s32[8,8]{1,0:T(8,128)}, u32[]{:S(2)}) copy-start(s32[8,8]{1,0:T(8,128)} %param.12) | copy-start | bytes 772
  11.4 12.1 %copy-start.7 = (bf16[8,7168]{1,0:T(8,128)(2,1)S(1)}, bf16[8,7168]{1,0:T(8,128)(2,1)}, u32[]{:S(2)}) copy-start(bf16[8,7168]{1,0:T(8,128)(2,1)} %param.10) | copy-start | bytes 344068
  11.4 58.9 %all-to-all-start = ((bf16[128,2,7168]{2,1,0:T(2,128)(2,1)}), bf16[128,2,7168]{2,1,0:T(2,128)(2,1)}, u32[]{:S(2)}, u32[]{:S(2)}) async-start(bf16[128,2,7168]{2,1,0:T(2,128)(2,1)} %bitcast.57), calls=%async_computation | async-start | bytes 7340032 | tf_op jit(solution)/shard_map/all_to_all | solution.py:35
  74.0 52.8 %all-to-all-start.2 = ((bf16[128,2,7168]{2,1,0:T(2,128)(2,1)}), bf16[128,2,7168]{2,1,0:T(2,128)(2,1)}, u32[]{:S(2)}, u32[]{:S(2)}) async-start(bf16[128,2,7168]{2,1,0:T(2,128)(2,1)} %bitcast.58), calls=%async_computation.2 | async-start | bytes 7340032 | tf_op jit(solution)/shard_map/all_to_all | solution.py:36
  88.1 4.4 %copy-start = (bf16[256,7168]{1,0:T(8,128)(2,1)S(1)}, bf16[256,7168]{1,0:T(8,128)(2,1)}, u32[]{:S(2)}) copy-start(bf16[256,7168]{1,0:T(8,128)(2,1)} %reshape.134) | copy-start | bytes 11010052
  88.1 5.3 %copy-start.2 = (bf16[1,7168,256]{2,1,0:T(8,128)(2,1)S(1)}, bf16[1,7168,256]{2,1,0:T(8,128)(2,1)}, u32[]{:S(2)}) copy-start(bf16[1,7168,256]{2,1,0:T(8,128)(2,1)} %param.16) | copy-start | bytes 11010052
  135.2 4.5 %copy-start.4 = (bf16[1,7168,256]{2,1,0:T(8,128)(2,1)S(1)}, bf16[1,7168,256]{2,1,0:T(8,128)(2,1)}, u32[]{:S(2)}) copy-start(bf16[1,7168,256]{2,1,0:T(8,128)(2,1)} %param.15) | copy-start | bytes 11010052
  139.7 2.0 copy-start.3
  152.8 52.8 %all-to-all-start.3 = ((bf16[128,2,7168]{2,1,0:T(2,128)(2,1)}), bf16[128,2,7168]{2,1,0:T(2,128)(2,1)}, u32[]{:S(2)}, u32[]{:S(2)}) async-start(bf16[128,2,7168]{2,1,0:T(2,128)(2,1)} %reshape.141), calls=%async_computation.3 | async-start | bytes 7340032 | tf_op jit(solution)/shard_map/all_to_all | solution.py:53
  205.6 106.1 %all-to-all-start.1 = ((bf16[128,2,7168]{2,1,0:T(2,128)(2,1)}), bf16[128,2,7168]{2,1,0:T(2,128)(2,1)}, u32[]{:S(2)}, u32[]{:S(2)}) async-start(bf16[128,2,7168]{2,1,0:T(2,128)(2,1)} %reshape.135), calls=%async_computation.1 | async-start | bytes 7340032 | tf_op jit(solution)/shard_map/all_to_all | solution.py:52
  211.5 5.2 %copy-start.1 = (bf16[256,7168]{1,0:T(8,128)(2,1)S(1)}, bf16[256,7168]{1,0:T(8,128)(2,1)}, u32[]{:S(2)}) copy-start(bf16[256,7168]{1,0:T(8,128)(2,1)} %reshape.134) | copy-start | bytes 11010052
  233.9 1.8 copy-start.5
  233.9 1.8 copy-start.6
where the time goes:
time: 328 us; the launch traced here: 326 us
  waiting for transfers between devices  111 us (34%)
  blocking collectives  75 us (23%)
  local copies, waits for them, and re-layouts  65.7 us (20%)
  matrix products  30.3 us (9%)
  starting transfers between devices  29.1 us (9%)
  other arithmetic  14.5 us (4%)
    unnamed x1, blocking collectives  75 us
    all_to_all x1, waiting for transfers between devices, dispatch(): lax.all_to_all(spread(send_normed), ('seq', 'ep'), split_axis=0, concat_a...  44.3 us
    all_to_all x1, waiting for transfers between devices, collect(): lax.all_to_all(shaped(back_part), ('seq', 'ep'), split_axis=0, concat_axi...  34 us
    all_to_all x1, waiting for transfers between devices, dispatch(): lax.all_to_all(spread(send_grad), ('seq', 'ep'), split_axis=0, concat_axi...  32.3 us
    reshape x2, local copies, waits for them, and re-layouts, folded(): values.astype(jnp.float32).reshape(seq_count, ep_count * capacity, width)  16.8 us
    reshape x2, local copies, waits for them, and re-layouts, dispatch(): return (got_normed.reshape(-1, width), got_grad.reshape(-1, width))  16.8 us
    reshape x2, local copies, waits for them, and re-layouts, shaped(): values.astype(jnp.bfloat16).reshape(seq_count * ep_count, capacity, width)  16.3 us
    all_to_all x1, starting transfers between devices, dispatch(): lax.all_to_all(spread(send_normed), ('seq', 'ep'), split_axis=0, concat_a...  11.9 us
  transfers between devices with their start and end apart: 4, of which 3 were waited for; matrix products, arithmetic and copies ran while one was open for 17% of the time, Pallas kernels for 0%

commit v1 on v0

v1 whole, which is shorter than its diff:
```python
import functools

import jax
import jax.numpy as jnp
from jax import lax
from jax.experimental import pallas as pl
from jax.experimental.pallas import tpu as pltpu
from jax.sharding import PartitionSpec as P

MESH = pl.DeviceIdType.MESH
RAMP = 8.0
GATE_UNIT = 65536.0
NORM_EPS = 1e-06

TOK = 8
TOP = 8
PAIRS = TOK * TOP
D = 7168
HID = 256
NX, NE = 4, 32
SEG = 4
WIDE = D // SEG
WA = 1152
WB = WIDE - WA
MSG = 512
BF = jnp.bfloat16
F32 = jnp.float32


def dot(a, b):
    return lax.dot_general(a, b, (((1,), (0,)), ((), ())), preferred_element_type=F32)


def dot_nt(a, b):
    return lax.dot_general(a, b, (((1,), (1,)), ((), ())), preferred_element_type=F32)


def dot_tn(a, b):
    return lax.dot_general(a, b, (((0,), (0,)), ((), ())), preferred_element_type=F32)


def iota(shape, dim):
    return lax.broadcasted_iota(jnp.int32, shape, dim)


def pair_table(routes_ref, gate_ref, ramp_ref, z, y, c):
    rep = (iota((PAIRS, TOK), 0) // TOP == iota((PAIRS, TOK), 1)).astype(F32)
    pick = iota((PAIRS, TOP), 0) % TOP == iota((PAIRS, TOP), 1)
    pick_t = iota((TOP, PAIRS), 1) % TOP == iota((TOP, PAIRS), 0)

    def column(v):
        return jnp.sum(jnp.where(pick, dot(rep, v), 0.0), axis=1, keepdims=True)

    routes = routes_ref[...].astype(F32)
    gate = gate_ref[...]
    route_col = column(routes)
    route_row = jnp.sum(
        jnp.where(pick_t, lax.dot_general(routes, rep, (((0,), (1,)), ((), ())), preferred_element_type=F32), 0.0),
        axis=0, keepdims=True)
    gate_col = column((gate >> 8).astype(F32)) * 256.0 + column((gate & 255).astype(F32))
    same = route_col.astype(jnp.int32) == iota((PAIRS, NE), 1)
    ramp_col = jnp.sum(jnp.where(same, ramp_ref[...].astype(F32), 0.0), axis=1, keepdims=True)
    coef = gate_col / GATE_UNIT * ramp_col / RAMP
    high = coef.astype(BF).astype(F32)
    low = coef - high

    before = (route_col == route_row) & (iota((PAIRS, PAIRS), 0) < iota((PAIRS, PAIRS), 1))
    row = jnp.sum(before.astype(F32), axis=0, keepdims=True).astype(jnp.int32)
    e = route_row.astype(jnp.int32)
    rel = (((e >> 3) - z) & 3) * 8 + ((((e >> 1) & 3) - y) & 3) * 2 + (((e & 1) - c) & 1)
    slot = (rel * 5) & 31
    place = (iota((PAIRS, PAIRS), 0) == slot * 2 + row).astype(BF)

    lane = iota((PAIRS, 128), 1)
    first, grad = lane < 64, ((lane >> 3) & 1) == 1
    mine = (iota((PAIRS, 128), 0) // TOP) == (lane & 7)
    value = jnp.where(first, jnp.where(grad, high, 1.0), jnp.where(grad, low, 0.0))
    return dot(place, jnp.where(mine, value, 0.0).astype(BF)).astype(BF)


def spread_table(pairs):
    m = iota((MSG, PAIRS), 0)
    expand = ((m >> 4) * 2 + (m & 1) == iota((MSG, PAIRS), 1)).astype(BF)
    m, lane = iota((MSG, 128), 0), iota((MSG, 128), 1)
    keep = (((m >> 2) & 3) == ((lane >> 4) & 3)) & (((m >> 1) & 1) == ((lane >> 3) & 1))
    return jnp.where(keep, dot(expand, pairs), 0.0).astype(BF)


def shuffles():
    def table(o, m):
        return (((o >> 1) & 15) * 16 + ((o >> 5) & 3) * 4 + (o >> 7) * 2 + (o & 1) == m).astype(BF)

    shape = (256, 256)
    return table(iota(shape, 0), iota(shape, 1)), table(iota(shape, 1), iota(shape, 0))


def layer(
    tok_ref, og_ref, routes_ref, gate_ref, ramp_ref, gain_ref, wg_hbm, wu_hbm, wd_hbm,
    mixed_ref, tg_ref, gq_ref, x_hbm, g_hbm, h_ref, gp_ref, up_ref,
    wg, wu, wd, tab, tbm, spread, perm, perm_t, sa, ra, sb, rb, xs, gs, acc, st_a, st_b,
    qa, qb, half1, half3, l1, l3, ca, cb, ys, xb, ng, mx, gsend, gx, gpart, gl,
    w_sem, out_sem, tb_s, tb_r, sa_s, sa_r, fw_s, fw_r, f2_s, f2_r, sb_s, sb_r,
    hf_s, hf_r, l_s, l_r, qb_s, qb_r, ca_s, ca_r, ys_s, ys_r, gx_s, gx_r, gl_s, gl_r,
):
    sx = lax.axis_index("seq")
    me = lax.axis_index("ep")
    z, y, c = me // 8, lax.rem(me // 2, 4), lax.rem(me, 2)

    def along(step):
        return {"seq": lax.rem(sx + step, 4)}

    def peer(i, back):
        b = lax.rem(i * 13, 32)
        dz, dy, dc = b // 8, lax.rem(b // 2, 4), lax.rem(b, 2)
        if back:
            dz, dy = 4 - dz, 4 - dy
        return {"ep": lax.rem(z + dz, 4) * 8 + lax.rem(y + dy, 4) * 2 + lax.rem(c + dc, 2)}

    def remote(src, dst, send, recv, to):
        return pltpu.make_async_remote_copy(src, dst, send, recv, device_id=to, device_id_type=MESH)

    barrier = pltpu.get_barrier_semaphore()
    for step in (1, 2, 3):
        pl.semaphore_signal(barrier, inc=1, device_id=along(step), device_id_type=MESH)

    def greet(i, _):
        pl.semaphore_signal(barrier, inc=1, device_id=peer(i, False), device_id_type=MESH)
        return 0

    lax.fori_loop(1, NE, greet, 0)

    loads = [pltpu.make_async_copy(a, b, w_sem.at[i]) for i, (a, b) in enumerate(((wg_hbm, wg), (wu_hbm, wu), (wd_hbm, wd)))]
    for load in loads:
        load.start()

    tokens = tok_ref[...].astype(F32)
    recip = lax.rsqrt(jnp.sum(tokens * tokens, axis=1, keepdims=True) / D + NORM_EPS)
    for s in range(SEG):
        cols = slice(s * WIDE, (s + 1) * WIDE)
        normed = tok_ref[:, cols].astype(F32) * recip * gain_ref[:, cols]
        both = jnp.concatenate([normed, og_ref[:, cols].astype(F32)], axis=0).astype(BF)
        tab[16 * s:16 * s + 16, :] = both
        tab[64 + 16 * s:80 + 16 * s, :] = both
    pairs = pair_table(routes_ref, gate_ref, ramp_ref, z, y, c)
    tbm[0, :, 0:WB] = tab[0:64, WA:WIDE]
    tbm[0, :, WB:WB + 128] = pairs
    pl.semaphore_wait(barrier, 34)

    tb_copies = [remote(tbm.at[0], tbm.at[step], tb_s.at[step - 1], tb_r.at[step - 1], along(step)) for step in (1, 2, 3)]
    for copy in tb_copies:
        copy.start()

    spread[0] = spread_table(pairs)
    for chunk in range(4):
        rows = slice(128 * chunk, 128 * chunk + 128)
        sa[rows, :] = dot(spread[0, rows, :], tab[:, 0:WA]).astype(BF)

        def send_a(i, _, chunk=chunk):
            at = pl.ds(pl.multiple_of(16 * i, 16), 16)
            remote(sa.at[at, :], ra.at[0, at, :], sa_s, sa_r.at[chunk], peer(i, False)).start()
            return 0

        lax.fori_loop(max(8 * chunk, 1), 8 * chunk + 8, send_a, 0)
    ra[0, 0:16, :] = sa[0:16, :]
    p, p_t = shuffles()
    perm[...] = p
    perm_t[...] = p_t

    for k in range(4):
        if k:
            tb_copies[k - 1].wait_recv()
            spread[k] = spread_table(tbm[k, :, WB:WB + 128])
        twice = jnp.concatenate([tbm[k, :, 0:WB]] * 2, axis=0)
        for chunk in range(4):
            rows = slice(128 * chunk, 128 * chunk + 128)
            sb[8 * chunk:8 * chunk + 8, 16 * k:16 * k + 16, :] = (
                dot(spread[k, rows, :], twice).astype(BF).reshape(8, 16, WB))

    def send_b(i, _):
        remote(sb.at[i], rb.at[i], sb_s, sb_r, peer(i, False)).start()
        return 0

    lax.fori_loop(1, NE, send_b, 0)
    rb[0] = sb[0]

    forward = []
    for chunk in range(4):
        rows = pl.ds(128 * chunk, 128)
        skip = 16 if chunk == 0 else 0
        got = pl.ds(128 * chunk + skip, 128 - skip)
        remote(sa.at[got, :], ra.at[0, got, :], sa_s, sa_r.at[chunk], along(1)).wait_recv()
        for way, (step, land) in enumerate(((1, 1), (3, 3))):
            k = 2 * chunk + way
            copy = remote(ra.at[0, rows, :], ra.at[land, rows, :], fw_s.at[k], fw_r.at[k], along(step))
            copy.start()
            forward.append(copy)

    def into_rows(value, row, col, width):
        out = dot(perm[...], value).astype(BF)
        for arr, ref in ((0, xs), (1, gs)):
            for s in range(SEG):
                at = (4 * arr + s) * 32
                ref[row:row + 32, s * WIDE + col:s * WIDE + col + width] = out[at:at + 32]

    def multiply(row, count, col, width):
        rows = slice(row, row + count)

        def one(s, _):
            cols = pl.ds(pl.multiple_of(s * WIDE + col, 128), width)
            left = xs[rows, cols]
            acc[0, rows, :] += dot(left, wg[cols, :])
            acc[1, rows, :] += dot(left, wu[cols, :])
            acc[2, rows, :] += dot_nt(gs[rows, cols], wd[:, cols])
            return 0

        lax.fori_loop(0, SEG, one, 0)

    acc[...] = jnp.zeros_like(acc)
    for load in loads:
        load.wait()

    def arrived(k):
        for g in range(2):
            into_rows(ra[k, 256 * g:256 * g + 256, :], 64 * k + 32 * g, 0, WA)
        multiply(64 * k, 64, 0, WA)

    arrived(0)
    further = []
    for chunk in range(4):
        for way in range(2):
            forward[2 * chunk + way].wait_recv()
        rows = pl.ds(128 * chunk, 128)
        land, step = (1, 1) if chunk < 2 else (3, 3)
        copy = remote(ra.at[land, rows, :], ra.at[2, rows, :], f2_s.at[chunk], f2_r.at[chunk], along(step))
        copy.start()
        further.append(copy)
    arrived(1)
    arrived(3)
    remote(sb.at[pl.ds(1, 31)], rb.at[pl.ds(1, 31)], sb_s, sb_r, along(1)).wait_recv()
    for k in range(4):
        for g in range(2):
            into_rows(rb[16 * g:16 * g + 16, 16 * k:16 * k + 16, :].reshape(256, WB), 64 * k + 32 * g, WA, WB)
    multiply(0, 256, WA, WB)
    for copy in further:
        copy.wait_recv()
    arrived(2)
    keep = [pltpu.make_async_copy(xs, x_hbm, out_sem.at[0]), pltpu.make_async_copy(gs, g_hbm, out_sem.at[1])]
    for copy in keep:
        copy.start()

    gate, up, back = acc[0], acc[1], acc[2]
    sig = jax.nn.sigmoid(gate)
    act = gate * sig
    h_ref[...] = (act * up).astype(BF)
    gp_ref[...] = (back * up * sig * (1.0 + gate * (1.0 - sig))).astype(BF)
    up_ref[...] = (back * act).astype(BF)

    def parts(k, col, width, st):
        rows = slice(64 * k, 64 * k + 64)

        def one(s, _):
            cols = pl.ds(pl.multiple_of(s * WIDE + col, 128), width)
            near = (dot_nt(gp_ref[rows, :], wg[cols, :]) + dot_nt(up_ref[rows, :], wu[cols, :])).astype(BF)
            far = dot(h_ref[rows, :], wd[:, cols]).astype(BF)
            for g in range(2):
                st[g, pl.ds(pl.multiple_of(32 * s, 32), 32), :] = near[32 * g:32 * g + 32]
                st[g, pl.ds(pl.multiple_of(128 + 32 * s, 32), 32), :] = far[32 * g:32 * g + 32]
            return 0

        lax.fori_loop(0, SEG, one, 0)

    def parts_a(k):
        parts(k, 0, WA, st_a)
        for g in range(2):
            qa[k, 256 * g:256 * g + 256, :] = dot(perm_t[...], st_a[g]).astype(BF)

    parts_a(2)
    low, high = pl.ds(0, 256), pl.ds(256, 256)
    halves = [
        remote(qa.at[2, low, :], half1, hf_s.at[0], hf_r.at[0], along(3)),
        remote(qa.at[2, high, :], half3, hf_s.at[1], hf_r.at[1], along(1)),
    ]
    for copy in halves:
        copy.start()
    for k in range(4):
        parts(k, WA, WB, st_b)
        for g in range(2):
            qb[16 * g:16 * g + 16, 16 * k:16 * k + 16, :] = dot(perm_t[...], st_b[g]).astype(BF).reshape(16, 16, WB)

    def return_b(i, _):
        remote(qb.at[i], cb.at[i], qb_s, qb_r, peer(i, True)).start()
        return 0

    lax.fori_loop(1, NE, return_b, 0)
    cb[0] = qb[0]

    sums = {}

    def send_sum(k, chunk):
        rows = pl.ds(128 * chunk, 128)
        land, step, way = (l1, 3, 0) if k == 1 else (l3, 1, 1)
        sem = 2 * chunk + way
        copy = remote(qa.at[k, rows, :], land.at[rows, :], l_s.at[sem], l_r.at[sem], along(step))
        copy.start()
        sums[k, chunk] = copy

    def add_half(k, chunk):
        rows = slice(128 * chunk, 128 * chunk + 128)
        other = half1[rows, :] if k == 1 else half3[128 * chunk - 256:128 * chunk - 128, :]
        qa[k, rows, :] = (qa[k, rows, :].astype(F32) + other.astype(F32)).astype(BF)

    parts_a(1)
    send_sum(1, 2)
    parts_a(3)
    send_sum(3, 0)
    halves[0].wait_recv()
    halves[1].wait_recv()
    add_half(1, 0)
    send_sum(1, 0)
    add_half(3, 2)
    send_sum(3, 2)
    send_sum(1, 3)
    send_sum(3, 1)
    add_half(1, 1)
    send_sum(1, 1)
    add_half(3, 3)
    send_sum(3, 3)
    parts_a(0)
    for chunk in (0, 2, 1, 3):
        rows = slice(128 * chunk, 128 * chunk + 128)
        sums[1, chunk].wait_recv()
        sums[3, chunk].wait_recv()
        total = qa[0, rows, :].astype(F32) + l1[rows, :].astype(F32) + l3[rows, :].astype(F32)
        qa[0, rows, :] = total.astype(BF)

        def return_a(i, _):
            at = pl.ds(pl.multiple_of(16 * i, 16), 16)
            remote(qa.at[0, at, :], ca.at[at, :], ca_s, ca_r, peer(i, True)).start()
            return 0

        lax.fori_loop(max(8 * chunk, 1), 8 * chunk + 8, return_a, 0)
    ca[0:16, :] = qa[0, 0:16, :]

    def fold(k, value):
        out = dot_tn(spread[k], value)
        return out[0:64] + out[64:128]

    remote(qb.at[pl.ds(1, 31)], cb.at[pl.ds(1, 31)], qb_s, qb_r, along(1)).wait_recv()
    ys_copies = []
    for k in (2, 1, 3):
        ys[k] = fold(k, cb[:, 16 * k:16 * k + 16, :].reshape(MSG, WB)).astype(BF)
        copy = remote(ys.at[k], xb.at[k], ys_s.at[k - 1], ys_r.at[k - 1], along(4 - k))
        copy.start()
        ys_copies.append(copy)
    mine_b = fold(0, cb[:, 0:16, :].reshape(MSG, WB))
    for copy in ys_copies:
        copy.wait_recv()
    for k in (1, 2, 3):
        mine_b = mine_b + xb[k].astype(F32)
    for s in range(SEG):
        cols = slice(s * WIDE + WA, (s + 1) * WIDE)
        ng[:, cols] = mine_b[16 * s:16 * s + 8]
        mx[:, cols] = mine_b[16 * s + 8:16 * s + 16]
    back_rows = pl.ds(16, MSG - 16)
    remote(qa.at[0, back_rows, :], ca.at[back_rows, :], ca_s, ca_r, along(1)).wait_recv()
    mine_a = fold(0, ca[...])
    for s in range(SEG):
        cols = slice(s * WIDE, s * WIDE + WA)
        ng[:, cols] = mine_a[16 * s:16 * s + 8]
        mx[:, cols] = mine_a[16 * s + 8:16 * s + 16]

    tokens = tok_ref[...].astype(F32)
    grad = ng[...]
    term = jnp.sum(grad * tokens * recip, axis=0, keepdims=True)
    gsend[...] = jnp.zeros_like(gsend)
    for j in range(D // 128):
        at = (j // 14) * 16 + j % 14
        gsend[at:at + 1, :] = term[:, 128 * j:128 * j + 128]

    def quarter(step):
        return gsend.at[pl.ds(pl.multiple_of(lax.rem(sx + step, 4) * 16, 16), 16), :]

    gx_copies = [remote(quarter(step), gx.at[step - 1], gx_s.at[step - 1], gx_r.at[step - 1], along(step)) for step in (1, 2, 3)]
    for copy in gx_copies:
        copy.start()
    mixed_ref[...] = mx[...].astype(BF)
    for copy in gx_copies:
        copy.wait_recv()
    gpart[...] = gsend[pl.ds(pl.multiple_of(sx * 16, 16), 16), :] + gx[0] + gx[1] + gx[2]

    def send_gain(i, _):
        remote(gpart, gl.at[i], gl_s, gl_r, peer(i, False)).start()
        return 0

    lax.fori_loop(1, NE, send_gain, 0)
    gl[0] = gpart[...]
    scaled = gain_ref[...] * grad
    inner = jnp.sum(scaled * tokens, axis=1, keepdims=True)
    tg_ref[...] = (recip * scaled - tokens * (recip * recip * recip * inner / D)).astype(BF)
    remote(gl.at[pl.ds(1, 31)], gl.at[pl.ds(1, 31)], gl_s, gl_r, along(1)).wait_recv()
    gq_ref[...] = jnp.sum(gl[...], axis=0)

    for copy in tb_copies + forward + further + halves + list(sums.values()) + ys_copies + gx_copies:
        copy.wait_send()
    remote(sa.at[back_rows, :], sa.at[back_rows, :], sa_s, sa_r.at[0], along(1)).wait_send()
    remote(sb.at[pl.ds(1, 31)], rb.at[pl.ds(1, 31)], sb_s, sb_r, along(1)).wait_send()
    remote(qb.at[pl.ds(1, 31)], cb.at[pl.ds(1, 31)], qb_s, qb_r, along(1)).wait_send()
    remote(qa.at[0, back_rows, :], ca.at[back_rows, :], ca_s, ca_r, along(1)).wait_send()
    remote(gl.at[pl.ds(1, 31)], gl.at[pl.ds(1, 31)], gl_s, gl_r, along(1)).wait_send()
    for copy in keep:
        copy.wait()


def on_device(tokens, out_grad, routes, gate_fixed, ramp_step, norm_gain, w_gate, w_up, w_down):
    vmem = pl.BlockSpec(memory_space=pltpu.VMEM)
    hbm = pl.BlockSpec(memory_space=pl.ANY)
    dma = pltpu.SemaphoreType.DMA
    outs = pl.pallas_call(
        layer,
        name="layer",
        out_shape=(
            jax.ShapeDtypeStruct((TOK, D), BF),
            jax.ShapeDtypeStruct((TOK, D), BF),
            jax.ShapeDtypeStruct((16, 128), F32),
            jax.ShapeDtypeStruct((256, D), BF),
            jax.ShapeDtypeStruct((256, D), BF),
            jax.ShapeDtypeStruct((256, HID), BF),
            jax.ShapeDtypeStruct((256, HID), BF),
            jax.ShapeDtypeStruct((256, HID), BF),
        ),
        in_specs=[vmem] * 6 + [hbm] * 3,
        out_specs=(vmem, vmem, vmem, hbm, hbm, vmem, vmem, vmem),
        scratch_shapes=[
            pltpu.VMEM((D, HID), BF), pltpu.VMEM((D, HID), BF), pltpu.VMEM((HID, D), BF),
            pltpu.VMEM((128, WIDE), BF),
            pltpu.VMEM((4, 64, WB + 128), BF),
            pltpu.VMEM((4, MSG, 128), BF),
            pltpu.VMEM((256, 256), BF), pltpu.VMEM((256, 256), BF),
            pltpu.VMEM((MSG, WA), BF), pltpu.VMEM((4, MSG, WA), BF),
            pltpu.VMEM((NE, 64, WB), BF), pltpu.VMEM((NE, 64, WB), BF),
            pltpu.VMEM((256, D), BF), pltpu.VMEM((256, D), BF),
            pltpu.VMEM((3, 256, HID), F32),
            pltpu.VMEM((2, 256, WA), BF), pltpu.VMEM((2, 256, WB), BF),
            pltpu.VMEM((4, MSG, WA), BF), pltpu.VMEM((NE, 64, WB), BF),
            pltpu.VMEM((256, WA), BF), pltpu.VMEM((256, WA), BF),
            pltpu.VMEM((MSG, WA), BF), pltpu.VMEM((MSG, WA), BF),
            pltpu.VMEM((MSG, WA), BF), pltpu.VMEM((NE, 64, WB), BF),
            pltpu.VMEM((4, 64, WB), BF), pltpu.VMEM((4, 64, WB), BF),
            pltpu.VMEM((TOK, D), F32), pltpu.VMEM((TOK, D), F32),
            pltpu.VMEM((64, 128), F32), pltpu.VMEM((3, 16, 128), F32),
            pltpu.VMEM((16, 128), F32), pltpu.VMEM((NE, 16, 128), F32),
            dma((3,)), dma((2,)), dma((3,)), dma((3,)), dma, dma((4,)), dma((8,)), dma((8,)), dma((4,)), dma((4,)), dma, dma,
            dma((2,)), dma((2,)), dma((8,)), dma((8,)), dma, dma, dma, dma, dma((3,)), dma((3,)), dma((3,)), dma((3,)), dma, dma,
        ],
        compiler_params=pltpu.CompilerParams(collective_id=0, has_side_effects=True, vmem_limit_bytes=60 * 2**20),
        cost_estimate=pl.CostEstimate(flops=8 * 10**9, bytes_accessed=20 * 10**6, transcendentals=65536),
    )(tokens, out_grad, routes, gate_fixed, ramp_step.reshape(1, NE), norm_gain.reshape(1, D), w_gate[0], w_up[0], w_down[0])
    mixed, tokens_grad, quarter, rows_x, rows_g, hidden, gate_pre, up_pre = outs
    gain_grad = lax.dynamic_slice(quarter.reshape(-1), (lax.axis_index("ep") * 56,), (56,))
    w_gate_grad = dot_tn(rows_x, gate_pre).astype(BF)[None]
    w_up_grad = dot_tn(rows_x, up_pre).astype(BF)[None]
    w_down_grad = dot_tn(hidden, rows_g).astype(BF)[None]
    return (mixed, tokens_grad, gain_grad, w_gate_grad, w_up_grad, w_down_grad)


def solution(mesh):
    return jax.shard_map(
        on_device,
        mesh=mesh,
        in_specs=(
            P(("seq", "ep"), None),
            P(("seq", "ep"), None),
            P(("seq", "ep"), None),
            P(("seq", "ep"), None),
            P(),
            P(),
            P("ep", None, "seq"),
            P("ep", None, "seq"),
            P("ep", "seq", None),
        ),
        out_specs=(
            P(("seq", "ep"), None),
            P(("seq", "ep"), None),
            P(("seq", "ep")),
            P("ep", None, "seq"),
            P("ep", None, "seq"),
            P("ep", "seq", None),
        ),
        check_vma=False,
    )
```

time: 328 us -> 142 us (0.43)
  Pallas kernels: 0 us -> 127 us
  waiting for transfers between devices: 111 us -> 0 us
  blocking collectives: 75 us -> 0 us
  local copies, waits for them, and re-layouts: 65.7 us -> 2.6 us
  starting transfers between devices: 29.1 us -> 0 us
  matrix products: 30.3 us -> 11.2 us
  other arithmetic: 14.5 us -> 0 us
    pallas_call x0 -> x1, Pallas kernels: none -> 127 us  [on_device(): pl.pallas_call(layer, name='layer', out_shape=(jax.ShapeDtypeStruct((TOK,...]
    all_to_all x4 -> x0, waiting for transfers between devices: 111 us -> none  [the longest x1 44.3 us: dispatch(): lax.all_to_all(spread(send_normed), ('seq', 'ep'), split_axis=0, concat_a...]
    unnamed x1 -> x0, blocking collectives: 75 us -> none
    reshape x6 -> x0, local copies, waits for them, and re-layouts: 49.8 us -> none  [the longest x2 16.8 us: folded(): values.astype(jnp.float32).reshape(seq_count, ep_count * capacity, width)]
    all_to_all x4 -> x0, starting transfers between devices: 29.1 us -> none  [the longest x1 11.9 us: dispatch(): lax.all_to_all(spread(send_normed), ('seq', 'ep'), split_axis=0, concat_a...]
    dot_general x9 -> x3, matrix products: 30.3 us -> 11.2 us  [dot_tn(): lax.dot_general(a, b, (((0,), (0,)), ((), ())), preferred_element_type=F32)]
    reduce_sum x7 -> x0, other arithmetic: 9.68 us -> none  [the longest x2 5.52 us: folded(): return jnp.sum(wide, axis=0).astype(jnp.bfloat16)]
    broadcast_in_dim x4 -> x0, local copies, waits for them, and re-layouts: 8.14 us -> none  [spread(): jnp.broadcast_to(buffer.reshape(1, experts, capacity, width), (seq_count,...]
  transfers between devices with their start and end apart: 4 -> 0, of which waited for: 3 -> 0; matrix products, arithmetic and copies ran while one was open for 17% -> 0% of each run, Pallas kernels for 0% -> 0%
where the time goes in v1:
time: 142 us; the launch traced here: 141 us
  Pallas kernels  127 us (89%)
  matrix products  11.2 us (8%)
  local copies, waits for them, and re-layouts  2.6 us (2%)
    pallas_call x1, Pallas kernels, on_device(): pl.pallas_call(layer, name='layer', out_shape=(jax.ShapeDtypeStruct((TOK,...  127 us
    dot_general x3, matrix products, dot_tn(): lax.dot_general(a, b, (((0,), (0,)), ((), ())), preferred_element_type=F32)  11.2 us

profile of v1, /device:TPU:1, one launch (start us, length us, event | category | flops | bytes accessed | tf_op | source)
XLA Modules:
  0.0 141.4 jit_solution(2886219675337169675)
XLA Ops:
  0.6 126.9 %layer.1 = (bf16[8,7168]{1,0:T(8,128)(2,1)}, bf16[8,7168]{1,0:T(8,128)(2,1)}, f32[16,128]{1,0:T(8,128)}, bf16[256,7168]{1,0:T(8,128)(2,1)}, bf16[256,7168]{1,0:T...) custom-call(bf16[8,7168]{1,0:T(8,128)(2,1)} %tok_ref.1, ...), custom_call_target="tpu_custom_call" | custom-call | flops 8000000000 | bytes 20000000 | tf_op jit(solution)/shard_map/layer/pallas_call | solution.py:418
  127.6 1.3 dynamic_slice.3
  128.9 0.0 copy-start
  128.9 0.0 copy-start.3
  128.9 5.2 %fusion = bf16[1,7168,256]{2,1,0:T(8,128)(2,1)} fusion(bf16[256,7168]{1,0:T(8,128)(2,1)} %get-tuple-element.17, bf16[256,256]{1,0:T(8,128)(2,1)} %get-tuple-element.18), kind=kOutput, calls=%fused_computation.3 | convolution fusion | flops 941359104 | bytes 7471104 | tf_op jit(solution)/shard_map/dot_general | solution.py:39
  134.1 0.0 copy-done
  134.1 0.0 copy-done.3
  134.1 0.0 copy-start.1
  134.1 0.0 copy-start.2
  134.1 3.0 %fusion.1 = bf16[1,7168,256]{2,1,0:T(8,128)(2,1)} fusion(bf16[256,7168]{1,0:T(8,128)(2,1)S(1)} %copy-done, bf16[256,256]{1,0:T(8,128)(2,1)S(1)} %copy-done.3), kind=kOutput, calls=%fused_computation.4 | convolution fusion | flops 941359104 | bytes 7471104 | tf_op jit(solution)/shard_map/dot_general | solution.py:39
  137.1 0.0 copy-done.1
  137.1 0.0 copy-done.2
  137.1 0.0 copy-start.5
  137.1 0.0 copy-start.4
  137.1 3.0 %fusion.2 = bf16[1,256,7168]{2,1,0:T(8,128)(2,1)} fusion(bf16[256,256]{1,0:T(8,128)(2,1)S(1)} %copy-done.2, bf16[256,7168]{1,0:T(8,128)(2,1)S(1)} %copy-done.1), kind=kOutput, calls=%fused_computation.5 | convolution fusion | flops 941359104 | bytes 7471104 | tf_op jit(solution)/shard_map/dot_general | solution.py:39
  140.1 0.0 copy-done.5
  140.1 0.6 copy.17
  140.7 0.0 copy-done.4
  140.7 0.6 copy.18
Async XLA Ops:
  128.9 5.2 %copy-start = (bf16[256,7168]{1,0:T(8,128)(2,1)S(1)}, bf16[256,7168]{1,0:T(8,128)(2,1)}, u32[]{:S(2)}) copy-start(bf16[256,7168]{1,0:T(8,128)(2,1)} %get-tuple-element.17) | copy-start | bytes 11010052
  128.9 5.2 %copy-start.3 = (bf16[256,256]{1,0:T(8,128)(2,1)S(1)}, bf16[256,256]{1,0:T(8,128)(2,1)}, u32[]{:S(2)}) copy-start(bf16[256,256]{1,0:T(8,128)(2,1)} %get-tuple-element.19) | copy-start | bytes 393220
  134.1 3.0 %copy-start.1 = (bf16[256,7168]{1,0:T(8,128)(2,1)S(1)}, bf16[256,7168]{1,0:T(8,128)(2,1)}, u32[]{:S(2)}) copy-start(bf16[256,7168]{1,0:T(8,128)(2,1)} %get-tuple-element.21) | copy-start | bytes 11010052
  134.1 3.0 %copy-start.2 = (bf16[256,256]{1,0:T(8,128)(2,1)S(1)}, bf16[256,256]{1,0:T(8,128)(2,1)}, u32[]{:S(2)}) copy-start(bf16[256,256]{1,0:T(8,128)(2,1)} %get-tuple-element.20) | copy-start | bytes 393220
  137.1 3.0 %copy-start.5 = (bf16[8,7168]{1,0:T(8,128)(2,1)S(1)}, bf16[8,7168]{1,0:T(8,128)(2,1)}, u32[]{:S(2)}) copy-start(bf16[8,7168]{1,0:T(8,128)(2,1)} %get-tuple-element.28) | copy-start | bytes 344068
  137.1 3.6 %copy-start.4 = (bf16[8,7168]{1,0:T(8,128)(2,1)S(1)}, bf16[8,7168]{1,0:T(8,128)(2,1)}, u32[]{:S(2)}) copy-start(bf16[8,7168]{1,0:T(8,128)(2,1)} %get-tuple-element.29) | copy-start | bytes 344068

commit v2 on v1

--- a/solution.py
+++ b/solution.py
@@ -23,6 +23,7 @@
 WA = 1152
 WB = WIDE - WA
 MSG = 512
+PLACE = {0: 0, 1: 1, 3: 2, 2: 3}
 BF = jnp.bfloat16
 F32 = jnp.float32
 
@@ -98,7 +99,7 @@
     tok_ref, og_ref, routes_ref, gate_ref, ramp_ref, gain_ref, wg_hbm, wu_hbm, wd_hbm,
     mixed_ref, tg_ref, gq_ref, x_hbm, g_hbm, h_ref, gp_ref, up_ref,
     wg, wu, wd, tab, tbm, spread, perm, perm_t, sa, ra, sb, rb, xs, gs, acc, st_a, st_b,
-    qa, qb, half1, half3, l1, l3, ca, cb, ys, xb, ng, mx, gsend, gx, gpart, gl,
+    qa, qb, half1, half3, l1, l3, ca, cb, ys, xb, ng, mx, gacc, gsend, gx, gpart, gl,
     w_sem, out_sem, tb_s, tb_r, sa_s, sa_r, fw_s, fw_r, f2_s, f2_r, sb_s, sb_r,
     hf_s, hf_r, l_s, l_r, qb_s, qb_r, ca_s, ca_r, ys_s, ys_r, gx_s, gx_r, gl_s, gl_r,
 ):
@@ -166,25 +167,9 @@
     perm[...] = p
     perm_t[...] = p_t
 
-    for k in range(4):
-        if k:
-            tb_copies[k - 1].wait_recv()
-            spread[k] = spread_table(tbm[k, :, WB:WB + 128])
-        twice = jnp.concatenate([tbm[k, :, 0:WB]] * 2, axis=0)
-        for chunk in range(4):
-            rows = slice(128 * chunk, 128 * chunk + 128)
-            sb[8 * chunk:8 * chunk + 8, 16 * k:16 * k + 16, :] = (
-                dot(spread[k, rows, :], twice).astype(BF).reshape(8, 16, WB))
-
-    def send_b(i, _):
-        remote(sb.at[i], rb.at[i], sb_s, sb_r, peer(i, False)).start()
-        return 0
-
-    lax.fori_loop(1, NE, send_b, 0)
-    rb[0] = sb[0]
-
     forward = []
-    for chunk in range(4):
+
+    def send_forward(chunk):
         rows = pl.ds(128 * chunk, 128)
         skip = 16 if chunk == 0 else 0
         got = pl.ds(128 * chunk + skip, 128 - skip)
@@ -195,6 +180,40 @@
             copy.start()
             forward.append(copy)
 
+    def make_b(k):
+        if k:
+            tb_copies[k - 1].wait_recv()
+            spread[k] = spread_table(tbm[k, :, WB:WB + 128])
+        twice = jnp.concatenate([tbm[k, :, 0:WB]] * 2, axis=0)
+        at = 16 * PLACE[k]
+        for chunk in range(4):
+            rows = slice(128 * chunk, 128 * chunk + 128)
+            sb[8 * chunk:8 * chunk + 8, at:at + 16, :] = dot(spread[k, rows, :], twice).astype(BF).reshape(8, 16, WB)
+
+    early, late = pl.ds(0, 48), pl.ds(48, 16)
+
+    def over_plane(src, dst, part, send, recv, back):
+        def one(i, _):
+            remote(src.at[i, part, :], dst.at[i, part, :], send, recv, peer(i, back)).start()
+            return 0
+
+        lax.fori_loop(1, NE, one, 0)
+
+    def whole(src, dst, part, send, recv):
+        return remote(src.at[pl.ds(1, 31), part, :], dst.at[pl.ds(1, 31), part, :], send, recv, along(1))
+
+    make_b(0)
+    send_forward(0)
+    make_b(1)
+    make_b(3)
+    over_plane(sb, rb, early, sb_s.at[0], sb_r.at[0], False)
+    send_forward(1)
+    make_b(2)
+    over_plane(sb, rb, late, sb_s.at[1], sb_r.at[1], False)
+    rb[0] = sb[0]
+    send_forward(2)
+    send_forward(3)
+
     def into_rows(value, row, col, width):
         out = dot(perm[...], value).astype(BF)
         for arr, ref in ((0, xs), (1, gs)):
@@ -219,48 +238,54 @@
     for load in loads:
         load.wait()
 
-    def arrived(k):
+    def sort_a(k):
         for g in range(2):
-            into_rows(ra[k, 256 * g:256 * g + 256, :], 64 * k + 32 * g, 0, WA)
-        multiply(64 * k, 64, 0, WA)
-
-    arrived(0)
+            into_rows(ra[k, 256 * g:256 * g + 256, :], 64 * PLACE[k] + 32 * g, 0, WA)
+
+    def sort_b(k):
+        at = 16 * PLACE[k]
+        for g in range(2):
+            into_rows(rb[16 * g:16 * g + 16, at:at + 16, :].reshape(256, WB), 64 * PLACE[k] + 32 * g, WA, WB)
+
+    def activate(row, count):
+        rows = slice(row, row + count)
+        gate, up, back = acc[0, rows, :], acc[1, rows, :], acc[2, rows, :]
+        sig = jax.nn.sigmoid(gate)
+        act = gate * sig
+        h_ref[rows, :] = (act * up).astype(BF)
+        gp_ref[rows, :] = (back * up * sig * (1.0 + gate * (1.0 - sig))).astype(BF)
+        up_ref[rows, :] = (back * act).astype(BF)
+
+    sort_a(0)
+    multiply(0, 64, 0, WA)
     further = []
     for chunk in range(4):
-        for way in range(2):
-            forward[2 * chunk + way].wait_recv()
+        land, step, way = (1, 1, 0) if chunk < 2 else (3, 3, 1)
+        forward[2 * chunk + way].wait_recv()
         rows = pl.ds(128 * chunk, 128)
-        land, step = (1, 1) if chunk < 2 else (3, 3)
         copy = remote(ra.at[land, rows, :], ra.at[2, rows, :], f2_s.at[chunk], f2_r.at[chunk], along(step))
         copy.start()
         further.append(copy)
-    arrived(1)
-    arrived(3)
-    remote(sb.at[pl.ds(1, 31)], rb.at[pl.ds(1, 31)], sb_s, sb_r, along(1)).wait_recv()
-    for k in range(4):
-        for g in range(2):
-            into_rows(rb[16 * g:16 * g + 16, 16 * k:16 * k + 16, :].reshape(256, WB), 64 * k + 32 * g, WA, WB)
-    multiply(0, 256, WA, WB)
-    for copy in further:
-        copy.wait_recv()
-    arrived(2)
-    keep = [pltpu.make_async_copy(xs, x_hbm, out_sem.at[0]), pltpu.make_async_copy(gs, g_hbm, out_sem.at[1])]
-    for copy in keep:
-        copy.start()
-
-    gate, up, back = acc[0], acc[1], acc[2]
-    sig = jax.nn.sigmoid(gate)
-    act = gate * sig
-    h_ref[...] = (act * up).astype(BF)
-    gp_ref[...] = (back * up * sig * (1.0 + gate * (1.0 - sig))).astype(BF)
-    up_ref[...] = (back * act).astype(BF)
+    for chunk in range(4):
+        forward[2 * chunk + (1 if chunk < 2 else 0)].wait_recv()
+    sort_a(1)
+    sort_a(3)
+    multiply(64, 128, 0, WA)
+    whole(sb, rb, early, sb_s.at[0], sb_r.at[0]).wait_recv()
+    for k in (0, 1, 3):
+        sort_b(k)
+    multiply(0, 192, WA, WB)
+    activate(0, 192)
 
     def parts(k, col, width, st):
-        rows = slice(64 * k, 64 * k + 64)
+        row = 64 * PLACE[k]
+        rows = slice(row, row + 64)
 
         def one(s, _):
             cols = pl.ds(pl.multiple_of(s * WIDE + col, 128), width)
-            near = (dot_nt(gp_ref[rows, :], wg[cols, :]) + dot_nt(up_ref[rows, :], wu[cols, :])).astype(BF)
+            near = dot_nt(gp_ref[rows, :], wg[cols, :]) + dot_nt(up_ref[rows, :], wu[cols, :])
+            gacc[:, cols] += jnp.sum((near * xs[rows, cols].astype(F32)).reshape(8, 8, width), axis=0)
+            near = near.astype(BF)
             far = dot(h_ref[rows, :], wd[:, cols]).astype(BF)
             for g in range(2):
                 st[g, pl.ds(pl.multiple_of(32 * s, 32), 32), :] = near[32 * g:32 * g + 32]
@@ -274,6 +299,49 @@
         for g in range(2):
             qa[k, 256 * g:256 * g + 256, :] = dot(perm_t[...], st_a[g]).astype(BF)
 
+    def parts_b(k):
+        parts(k, WA, WB, st_b)
+        at = 16 * PLACE[k]
+        for g in range(2):
+            qb[16 * g:16 * g + 16, at:at + 16, :] = dot(perm_t[...], st_b[g]).astype(BF).reshape(16, 16, WB)
+
+    gacc[...] = jnp.zeros_like(gacc)
+    for k in (0, 1, 3):
+        parts_b(k)
+    over_plane(qb, cb, early, qb_s.at[0], qb_r.at[0], True)
+
+    sums = {}
+
+    def send_sum(k, chunk):
+        rows = pl.ds(128 * chunk, 128)
+        land, step, way = (l1, 3, 0) if k == 1 else (l3, 1, 1)
+        sem = 2 * chunk + way
+        copy = remote(qa.at[k, rows, :], land.at[rows, :], l_s.at[sem], l_r.at[sem], along(step))
+        copy.start()
+        sums[k, chunk] = copy
+
+    def add_half(k, chunk):
+        rows = slice(128 * chunk, 128 * chunk + 128)
+        other = half1[rows, :] if k == 1 else half3[128 * chunk - 256:128 * chunk - 128, :]
+        qa[k, rows, :] = (qa[k, rows, :].astype(F32) + other.astype(F32)).astype(BF)
+
+    parts_a(1)
+    send_sum(1, 2)
+    send_sum(1, 3)
+    parts_a(3)
+    send_sum(3, 0)
+    send_sum(3, 1)
+
+    for copy in further:
+        copy.wait_recv()
+    sort_a(2)
+    whole(sb, rb, late, sb_s.at[1], sb_r.at[1]).wait_recv()
+    sort_b(2)
+    multiply(192, 64, 0, WIDE)
+    activate(192, 64)
+    keep = [pltpu.make_async_copy(xs, x_hbm, out_sem.at[0]), pltpu.make_async_copy(gs, g_hbm, out_sem.at[1])]
+    for copy in keep:
+        copy.start()
     parts_a(2)
     low, high = pl.ds(0, 256), pl.ds(256, 256)
     halves = [
@@ -282,51 +350,45 @@
     ]
     for copy in halves:
         copy.start()
-    for k in range(4):
-        parts(k, WA, WB, st_b)
-        for g in range(2):
-            qb[16 * g:16 * g + 16, 16 * k:16 * k + 16, :] = dot(perm_t[...], st_b[g]).astype(BF).reshape(16, 16, WB)
-
-    def return_b(i, _):
-        remote(qb.at[i], cb.at[i], qb_s, qb_r, peer(i, True)).start()
-        return 0
-
-    lax.fori_loop(1, NE, return_b, 0)
+    parts_b(2)
+    over_plane(qb, cb, late, qb_s.at[1], qb_r.at[1], True)
     cb[0] = qb[0]
-
-    sums = {}
-
-    def send_sum(k, chunk):
-        rows = pl.ds(128 * chunk, 128)
-        land, step, way = (l1, 3, 0) if k == 1 else (l3, 1, 1)
-        sem = 2 * chunk + way
-        copy = remote(qa.at[k, rows, :], land.at[rows, :], l_s.at[sem], l_r.at[sem], along(step))
+    parts_a(0)
+
+    term = jnp.sum(gacc[...], axis=0, keepdims=True) / gain_ref[...]
+    gsend[...] = jnp.zeros_like(gsend)
+    for j in range(D // 128):
+        at = (j // 14) * 16 + j % 14
+        gsend[at:at + 1, :] = term[:, 128 * j:128 * j + 128]
+
+    def quarter(step):
+        return gsend.at[pl.ds(pl.multiple_of(lax.rem(sx + step, 4) * 16, 16), 16), :]
+
+    gx_copies = [remote(quarter(step), gx.at[step - 1], gx_s.at[step - 1], gx_r.at[step - 1], along(step)) for step in (1, 2, 3)]
+    for copy in gx_copies:
         copy.start()
-        sums[k, chunk] = copy
-
-    def add_half(k, chunk):
-        rows = slice(128 * chunk, 128 * chunk + 128)
-        other = half1[rows, :] if k == 1 else half3[128 * chunk - 256:128 * chunk - 128, :]
-        qa[k, rows, :] = (qa[k, rows, :].astype(F32) + other.astype(F32)).astype(BF)
-
-    parts_a(1)
-    send_sum(1, 2)
-    parts_a(3)
-    send_sum(3, 0)
     halves[0].wait_recv()
     halves[1].wait_recv()
     add_half(1, 0)
     send_sum(1, 0)
     add_half(3, 2)
     send_sum(3, 2)
-    send_sum(1, 3)
-    send_sum(3, 1)
     add_half(1, 1)
     send_sum(1, 1)
     add_half(3, 3)
     send_sum(3, 3)
-    parts_a(0)
+
+    def send_gain(i, _):
+        remote(gpart, gl.at[i], gl_s, gl_r, peer(i, False)).start()
+        return 0
+
     for chunk in (0, 2, 1, 3):
+        if chunk == 1:
+            for copy in gx_copies:
+                copy.wait_recv()
+            gpart[...] = gsend[pl.ds(pl.multiple_of(sx * 16, 16), 16), :] + gx[0] + gx[1] + gx[2]
+            lax.fori_loop(1, NE, send_gain, 0)
+            gl[0] = gpart[...]
         rows = slice(128 * chunk, 128 * chunk + 128)
         sums[1, chunk].wait_recv()
         sums[3, chunk].wait_recv()
@@ -345,15 +407,21 @@
         out = dot_tn(spread[k], value)
         return out[0:64] + out[64:128]
 
-    remote(qb.at[pl.ds(1, 31)], cb.at[pl.ds(1, 31)], qb_s, qb_r, along(1)).wait_recv()
-    ys_copies = []
-    for k in (2, 1, 3):
-        ys[k] = fold(k, cb[:, 16 * k:16 * k + 16, :].reshape(MSG, WB)).astype(BF)
-        copy = remote(ys.at[k], xb.at[k], ys_s.at[k - 1], ys_r.at[k - 1], along(4 - k))
-        copy.start()
-        ys_copies.append(copy)
+    whole(qb, cb, early, qb_s.at[0], qb_r.at[0]).wait_recv()
+    ys_copies = {}
+
+    def give_back(k):
+        at = 16 * PLACE[k]
+        ys[k] = fold(k, cb[:, at:at + 16, :].reshape(MSG, WB)).astype(BF)
+        ys_copies[k] = remote(ys.at[k], xb.at[k], ys_s.at[k - 1], ys_r.at[k - 1], along(4 - k))
+        ys_copies[k].start()
+
+    give_back(1)
+    give_back(3)
     mine_b = fold(0, cb[:, 0:16, :].reshape(MSG, WB))
-    for copy in ys_copies:
+    whole(qb, cb, late, qb_s.at[1], qb_r.at[1]).wait_recv()
+    give_back(2)
+    for copy in ys_copies.values():
         copy.wait_recv()
     for k in (1, 2, 3):
         mine_b = mine_b + xb[k].astype(F32)
@@ -371,44 +439,46 @@
 
     tokens = tok_ref[...].astype(F32)
     grad = ng[...]
-    term = jnp.sum(grad * tokens * recip, axis=0, keepdims=True)
-    gsend[...] = jnp.zeros_like(gsend)
-    for j in range(D // 128):
-        at = (j // 14) * 16 + j % 14
-        gsend[at:at + 1, :] = term[:, 128 * j:128 * j + 128]
-
-    def quarter(step):
-        return gsend.at[pl.ds(pl.multiple_of(lax.rem(sx + step, 4) * 16, 16), 16), :]
-
-    gx_copies = [remote(quarter(step), gx.at[step - 1], gx_s.at[step - 1], gx_r.at[step - 1], along(step)) for step in (1, 2, 3)]
-    for copy in gx_copies:
-        copy.start()
     mixed_ref[...] = mx[...].astype(BF)
-    for copy in gx_copies:
-        copy.wait_recv()
-    gpart[...] = gsend[pl.ds(pl.multiple_of(sx * 16, 16), 16), :] + gx[0] + gx[1] + gx[2]
-
-    def send_gain(i, _):
-        remote(gpart, gl.at[i], gl_s, gl_r, peer(i, False)).start()
-        return 0
-
-    lax.fori_loop(1, NE, send_gain, 0)
-    gl[0] = gpart[...]
     scaled = gain_ref[...] * grad
     inner = jnp.sum(scaled * tokens, axis=1, keepdims=True)
     tg_ref[...] = (recip * scaled - tokens * (recip * recip * recip * inner / D)).astype(BF)
     remote(gl.at[pl.ds(1, 31)], gl.at[pl.ds(1, 31)], gl_s, gl_r, along(1)).wait_recv()
     gq_ref[...] = jnp.sum(gl[...], axis=0)
 
-    for copy in tb_copies + forward + further + halves + list(sums.values()) + ys_copies + gx_copies:
+    for copy in tb_copies + forward + further + halves + list(sums.values()) + list(ys_copies.values()) + gx_copies:
         copy.wait_send()
     remote(sa.at[back_rows, :], sa.at[back_rows, :], sa_s, sa_r.at[0], along(1)).wait_send()
-    remote(sb.at[pl.ds(1, 31)], rb.at[pl.ds(1, 31)], sb_s, sb_r, along(1)).wait_send()
-    remote(qb.at[pl.ds(1, 31)], cb.at[pl.ds(1, 31)], qb_s, qb_r, along(1)).wait_send()
+    for n, part in enumerate((early, late)):
+        whole(sb, rb, part, sb_s.at[n], sb_r.at[n]).wait_send()
+        whole(qb, cb, part, qb_s.at[n], qb_r.at[n]).wait_send()
     remote(qa.at[0, back_rows, :], ca.at[back_rows, :], ca_s, ca_r, along(1)).wait_send()
     remote(gl.at[pl.ds(1, 31)], gl.at[pl.ds(1, 31)], gl_s, gl_r, along(1)).wait_send()
     for copy in keep:
         copy.wait()
+
+
+def weight_grads(
+    x_ref, g_ref, h_ref, gp_ref, up_ref, quarter_ref, mixed_in, tg_in,
+    wg_ref, wu_ref, wd_ref, mixed_ref, tg_ref, gain_ref, turned,
+):
+    @pl.when(pl.program_id(0) == 0)
+    def _():
+        turned[...] = h_ref[...].T
+
+    turned_x = x_ref[...].T
+    wg_ref[0] = dot(turned_x, gp_ref[...]).astype(BF)
+    wu_ref[0] = dot(turned_x, up_ref[...]).astype(BF)
+    wd_ref[0] = dot(turned[...], g_ref[...]).astype(BF)
+    mixed_ref[...] = mixed_in[...]
+    tg_ref[...] = tg_in[...]
+
+    @pl.when(pl.program_id(0) == 0)
+    def _():
+        first = lax.axis_index("ep") * (D // 128)
+        row, lane = first // 128, lax.rem(first, 128)
+        two = jnp.concatenate([quarter_ref[pl.ds(row, 1), :], quarter_ref[pl.ds(row + 1, 1), :]], axis=1)
+        gain_ref[...] = pltpu.roll(two, lax.rem(256 - lane, 256), 1)[0, 0:D // 128]
 
 
 def on_device(tokens, out_grad, routes, gate_fixed, ramp_step, norm_gain, w_gate, w_up, w_down):
@@ -447,19 +517,38 @@
             pltpu.VMEM((MSG, WA), BF), pltpu.VMEM((NE, 64, WB), BF),
             pltpu.VMEM((4, 64, WB), BF), pltpu.VMEM((4, 64, WB), BF),
             pltpu.VMEM((TOK, D), F32), pltpu.VMEM((TOK, D), F32),
-            pltpu.VMEM((64, 128), F32), pltpu.VMEM((3, 16, 128), F32),
+            pltpu.VMEM((8, D), F32), pltpu.VMEM((64, 128), F32), pltpu.VMEM((3, 16, 128), F32),
             pltpu.VMEM((16, 128), F32), pltpu.VMEM((NE, 16, 128), F32),
-            dma((3,)), dma((2,)), dma((3,)), dma((3,)), dma, dma((4,)), dma((8,)), dma((8,)), dma((4,)), dma((4,)), dma, dma,
-            dma((2,)), dma((2,)), dma((8,)), dma((8,)), dma, dma, dma, dma, dma((3,)), dma((3,)), dma((3,)), dma((3,)), dma, dma,
+            dma((3,)), dma((2,)), dma((3,)), dma((3,)), dma, dma((4,)), dma((8,)), dma((8,)), dma((4,)), dma((4,)), dma((2,)), dma((2,)),
+            dma((2,)), dma((2,)), dma((8,)), dma((8,)), dma((2,)), dma((2,)), dma, dma, dma((3,)), dma((3,)), dma((3,)), dma((3,)), dma, dma,
         ],
         compiler_params=pltpu.CompilerParams(collective_id=0, has_side_effects=True, vmem_limit_bytes=60 * 2**20),
         cost_estimate=pl.CostEstimate(flops=8 * 10**9, bytes_accessed=20 * 10**6, transcendentals=65536),
     )(tokens, out_grad, routes, gate_fixed, ramp_step.reshape(1, NE), norm_gain.reshape(1, D), w_gate[0], w_up[0], w_down[0])
     mixed, tokens_grad, quarter, rows_x, rows_g, hidden, gate_pre, up_pre = outs
-    gain_grad = lax.dynamic_slice(quarter.reshape(-1), (lax.axis_index("ep") * 56,), (56,))
-    w_gate_grad = dot_tn(rows_x, gate_pre).astype(BF)[None]
-    w_up_grad = dot_tn(rows_x, up_pre).astype(BF)[None]
-    w_down_grad = dot_tn(hidden, rows_g).astype(BF)[None]
+    block = 1792
+    tall = pl.BlockSpec((1, block, HID), lambda i: (0, i, 0))
+    wide = pl.BlockSpec((256, block), lambda i: (0, i))
+    few = pl.BlockSpec((TOK, block), lambda i: (0, i))
+    fixed = pl.BlockSpec((256, HID), lambda i: (0, 0))
+    w_gate_grad, w_up_grad, w_down_grad, mixed, tokens_grad, gain_grad = pl.pallas_call(
+        weight_grads,
+        name="weight_grads",
+        grid=(D // block,),
+        out_shape=(
+            jax.ShapeDtypeStruct((1, D, HID), BF),
+            jax.ShapeDtypeStruct((1, D, HID), BF),
+            jax.ShapeDtypeStruct((1, HID, D), BF),
+            jax.ShapeDtypeStruct((TOK, D), BF),
+            jax.ShapeDtypeStruct((TOK, D), BF),
+            jax.ShapeDtypeStruct((D // 128,), F32),
+        ),
+        in_specs=[wide, wide, fixed, fixed, fixed, pl.BlockSpec((16, 128), lambda i: (0, 0)), few, few],
+        out_specs=(tall, tall, pl.BlockSpec((1, HID, block), lambda i: (0, 0, i)), few, few, pl.BlockSpec((D // 128,), lambda i: (0,))),
+        scratch_shapes=[pltpu.VMEM((HID, 256), BF)],
+        compiler_params=pltpu.CompilerParams(vmem_limit_bytes=60 * 2**20),
+        cost_estimate=pl.CostEstimate(flops=3 * 10**9, bytes_accessed=19 * 10**6, transcendentals=0),
+    )(rows_x, rows_g, hidden, gate_pre, up_pre, quarter, mixed, tokens_grad)
     return (mixed, tokens_grad, gain_grad, w_gate_grad, w_up_grad, w_down_grad)
 
 

time: 142 us -> 129 us (0.908)
  matrix products: 11.2 us -> 0 us
  local copies, waits for them, and re-layouts: 2.6 us -> 0 us
    dot_general x3 -> x0, matrix products: 11.2 us -> none  [dot_tn(): lax.dot_general(a, b, (((0,), (0,)), ((), ())), preferred_element_type=F32)]
    pallas_call x0 -> x1, Pallas kernels: none -> 9.56 us  [on_device(): pl.pallas_call(weight_grads, name='weight_grads', grid=(D // block,), out...]
    pallas_call x1, Pallas kernels: 127 us -> 119 us  [on_device(): pl.pallas_call(layer, name='layer', out_shape=(jax.ShapeDtypeStruct((TOK,...]
where the time goes in v2:
time: 129 us
  Pallas kernels  128 us (99%)
    pallas_call x1, Pallas kernels, on_device(): pl.pallas_call(layer, name='layer', out_shape=(jax.ShapeDtypeStruct((TOK,...  119 us
    pallas_call x1, Pallas kernels, on_device(): pl.pallas_call(weight_grads, name='weight_grads', grid=(D // block,), out...  9.56 us

profile of v2, /device:TPU:1, one launch (start us, length us, event | category | flops | bytes accessed | tf_op | source)
XLA Modules:
  0.0 129.2 jit_solution(16774731833704383281)
XLA Ops:
  0.6 118.8 %layer.1 = (bf16[8,7168]{1,0:T(8,128)(2,1)}, bf16[8,7168]{1,0:T(8,128)(2,1)}, f32[16,128]{1,0:T(8,128)}, bf16[256,7168]{1,0:T(8,128)(2,1)}, bf16[256,7168]{1,0:T...) custom-call(bf16[8,7168]{1,0:T(8,128)(2,1)} %tok_ref.1, ...), custom_call_target="tpu_custom_call" | custom-call | flops 8000000000 | bytes 20000000 | tf_op jit(solution)/shard_map/layer/pallas_call | solution.py:488
  119.5 9.6 %weight_grads.1 = (bf16[1,7168,256]{2,1,0:T(8,128)(2,1)}, bf16[1,7168,256]{2,1,0:T(8,128)(2,1)}, bf16[1,256,7168]{2,1,0:T(8,128)(2,1)}, bf16[8,7168]{1,0:T(8,128...) custom-call(bf16[256,7168]{1,0:T(8,128)(2,1)} %get-tuple-element.20.x_ref, bf16[256,7168]{1,0:T(8,128)(2,1)} %get-tuple-element.21.g_ref, ...), custom_call_target="tpu_custom_call" | custom-call | flops 3000000000 | bytes 19000000 | tf_op jit(solution)/shard_map/weight_grads/pallas_call | solution.py:534

commit v3 on v2

--- a/solution.py
+++ b/solution.py
@@ -20,9 +20,10 @@
 NX, NE = 4, 32
 SEG = 4
 WIDE = D // SEG
-WA = 1152
+WA = 1024
 WB = WIDE - WA
 MSG = 512
+HOP, HOP_BACK = 7, 23
 PLACE = {0: 0, 1: 1, 3: 2, 2: 3}
 BF = jnp.bfloat16
 F32 = jnp.float32
@@ -68,8 +69,9 @@
     before = (route_col == route_row) & (iota((PAIRS, PAIRS), 0) < iota((PAIRS, PAIRS), 1))
     row = jnp.sum(before.astype(F32), axis=0, keepdims=True).astype(jnp.int32)
     e = route_row.astype(jnp.int32)
-    rel = (((e >> 3) - z) & 3) * 8 + ((((e >> 1) & 3) - y) & 3) * 2 + (((e & 1) - c) & 1)
-    slot = (rel * 5) & 31
+    way = 1 - 2 * c
+    rel = ((((e >> 3) - z) * way) & 3) * 8 + (((((e >> 1) & 3) - y) * way) & 3) * 2 + (((e & 1) - c) & 1)
+    slot = (rel * HOP_BACK) & 31
     place = (iota((PAIRS, PAIRS), 0) == slot * 2 + row).astype(BF)
 
     lane = iota((PAIRS, 128), 1)
@@ -111,11 +113,10 @@
         return {"seq": lax.rem(sx + step, 4)}
 
     def peer(i, back):
-        b = lax.rem(i * 13, 32)
+        b = lax.rem(i * HOP, 32)
         dz, dy, dc = b // 8, lax.rem(b // 2, 4), lax.rem(b, 2)
-        if back:
-            dz, dy = 4 - dz, 4 - dy
-        return {"ep": lax.rem(z + dz, 4) * 8 + lax.rem(y + dy, 4) * 2 + lax.rem(c + dc, 2)}
+        way = 1 - 2 * lax.rem(c + dc + 1, 2) if back else 1 - 2 * c
+        return {"ep": lax.rem(z + 4 + way * dz, 4) * 8 + lax.rem(y + 4 + way * dy, 4) * 2 + lax.rem(c + dc, 2)}
 
     def remote(src, dst, send, recv, to):
         return pltpu.make_async_remote_copy(src, dst, send, recv, device_id=to, device_id_type=MESH)
@@ -526,7 +527,7 @@
         cost_estimate=pl.CostEstimate(flops=8 * 10**9, bytes_accessed=20 * 10**6, transcendentals=65536),
     )(tokens, out_grad, routes, gate_fixed, ramp_step.reshape(1, NE), norm_gain.reshape(1, D), w_gate[0], w_up[0], w_down[0])
     mixed, tokens_grad, quarter, rows_x, rows_g, hidden, gate_pre, up_pre = outs
-    block = 1792
+    block = 3584
     tall = pl.BlockSpec((1, block, HID), lambda i: (0, i, 0))
     wide = pl.BlockSpec((256, block), lambda i: (0, i))
     few = pl.BlockSpec((TOK, block), lambda i: (0, i))

time: 129 us -> 123 us (0.953)
  Pallas kernels: 128 us -> 121 us
    pallas_call x1, Pallas kernels: 119 us -> 113 us  [on_device(): pl.pallas_call(layer, name='layer', out_shape=(jax.ShapeDtypeStruct((TOK,...]
where the time goes in v3:
time: 123 us; the launch traced here: 122 us
  Pallas kernels  121 us (98%)
    pallas_call x1, Pallas kernels, on_device(): pl.pallas_call(layer, name='layer', out_shape=(jax.ShapeDtypeStruct((TOK,...  113 us
    pallas_call x1, Pallas kernels, on_device(): pl.pallas_call(weight_grads, name='weight_grads', grid=(D // block,), out...  8.68 us

profile of v3, /device:TPU:1, one launch (start us, length us, event | category | flops | bytes accessed | tf_op | source)
XLA Modules:
  0.0 122.1 jit_solution(301616440082995494)
XLA Ops:
  0.6 112.6 %layer.1 = (bf16[8,7168]{1,0:T(8,128)(2,1)}, bf16[8,7168]{1,0:T(8,128)(2,1)}, f32[16,128]{1,0:T(8,128)}, bf16[256,7168]{1,0:T(8,128)(2,1)}, bf16[256,7168]{1,0:T...) custom-call(bf16[8,7168]{1,0:T(8,128)(2,1)} %tok_ref.1, ...), custom_call_target="tpu_custom_call" | custom-call | flops 8000000000 | bytes 20000000 | tf_op jit(solution)/shard_map/layer/pallas_call | solution.py:489
  113.3 8.7 %weight_grads.1 = (bf16[1,7168,256]{2,1,0:T(8,128)(2,1)}, bf16[1,7168,256]{2,1,0:T(8,128)(2,1)}, bf16[1,256,7168]{2,1,0:T(8,128)(2,1)}, bf16[8,7168]{1,0:T(8,128...) custom-call(bf16[256,7168]{1,0:T(8,128)(2,1)} %get-tuple-element.20.x_ref, bf16[256,7168]{1,0:T(8,128)(2,1)} %get-tuple-element.21.g_ref, ...), custom_call_target="tpu_custom_call" | custom-call | flops 3000000000 | bytes 19000000 | tf_op jit(solution)/shard_map/weight_grads/pallas_call | solution.py:535

commit v4 on v3

--- a/solution.py
+++ b/solution.py
@@ -112,11 +112,17 @@
     def along(step):
         return {"seq": lax.rem(sx + step, 4)}
 
+    way = 1 - 2 * c
+    planes = [lax.rem(z + 4 + way * d, 4) * 8 for d in range(4)]
+    lines = [lax.rem(y + 4 + way * d, 4) * 2 for d in range(4)]
+    cores = [c, 1 - c]
+
     def peer(i, back):
-        b = lax.rem(i * HOP, 32)
-        dz, dy, dc = b // 8, lax.rem(b // 2, 4), lax.rem(b, 2)
-        way = 1 - 2 * lax.rem(c + dc + 1, 2) if back else 1 - 2 * c
-        return {"ep": lax.rem(z + 4 + way * dz, 4) * 8 + lax.rem(y + 4 + way * dy, 4) * 2 + lax.rem(c + dc, 2)}
+        b = i * HOP % 32
+        dz, dy, dc = b // 8, b // 2 % 4, b % 2
+        if back and dc == 0:
+            dz, dy = -dz % 4, -dy % 4
+        return {"ep": planes[dz] + lines[dy] + cores[dc]}
 
     def remote(src, dst, send, recv, to):
         return pltpu.make_async_remote_copy(src, dst, send, recv, device_id=to, device_id_type=MESH)
@@ -129,7 +135,8 @@
         pl.semaphore_signal(barrier, inc=1, device_id=peer(i, False), device_id_type=MESH)
         return 0
 
-    lax.fori_loop(1, NE, greet, 0)
+    for i in range(1, NE):
+        greet(i, 0)
 
     loads = [pltpu.make_async_copy(a, b, w_sem.at[i]) for i, (a, b) in enumerate(((wg_hbm, wg), (wu_hbm, wu), (wd_hbm, wd)))]
     for load in loads:
@@ -158,11 +165,12 @@
         sa[rows, :] = dot(spread[0, rows, :], tab[:, 0:WA]).astype(BF)
 
         def send_a(i, _, chunk=chunk):
-            at = pl.ds(pl.multiple_of(16 * i, 16), 16)
+            at = pl.ds(16 * i, 16)
             remote(sa.at[at, :], ra.at[0, at, :], sa_s, sa_r.at[chunk], peer(i, False)).start()
             return 0
 
-        lax.fori_loop(max(8 * chunk, 1), 8 * chunk + 8, send_a, 0)
+        for i in range(max(8 * chunk, 1), 8 * chunk + 8):
+            send_a(i, 0)
     ra[0, 0:16, :] = sa[0:16, :]
     p, p_t = shuffles()
     perm[...] = p
@@ -198,7 +206,8 @@
             remote(src.at[i, part, :], dst.at[i, part, :], send, recv, peer(i, back)).start()
             return 0
 
-        lax.fori_loop(1, NE, one, 0)
+        for i in range(1, NE):
+            one(i, 0)
 
     def whole(src, dst, part, send, recv):
         return remote(src.at[pl.ds(1, 31), part, :], dst.at[pl.ds(1, 31), part, :], send, recv, along(1))
@@ -388,7 +397,8 @@
             for copy in gx_copies:
                 copy.wait_recv()
             gpart[...] = gsend[pl.ds(pl.multiple_of(sx * 16, 16), 16), :] + gx[0] + gx[1] + gx[2]
-            lax.fori_loop(1, NE, send_gain, 0)
+            for i in range(1, NE):
+                send_gain(i, 0)
             gl[0] = gpart[...]
         rows = slice(128 * chunk, 128 * chunk + 128)
         sums[1, chunk].wait_recv()
@@ -397,11 +407,12 @@
         qa[0, rows, :] = total.astype(BF)
 
         def return_a(i, _):
-            at = pl.ds(pl.multiple_of(16 * i, 16), 16)
+            at = pl.ds(16 * i, 16)
             remote(qa.at[0, at, :], ca.at[at, :], ca_s, ca_r, peer(i, True)).start()
             return 0
 
-        lax.fori_loop(max(8 * chunk, 1), 8 * chunk + 8, return_a, 0)
+        for i in range(max(8 * chunk, 1), 8 * chunk + 8):
+            return_a(i, 0)
     ca[0:16, :] = qa[0, 0:16, :]
 
     def fold(k, value):

time: 123 us -> 122 us (level)
  no operation moved by 1% of the time
where the time goes in v4:
time: 122 us
  Pallas kernels  121 us (99%)
    pallas_call x1, Pallas kernels, on_device(): pl.pallas_call(layer, name='layer', out_shape=(jax.ShapeDtypeStruct((TOK,...  112 us
    pallas_call x1, Pallas kernels, on_device(): pl.pallas_call(weight_grads, name='weight_grads', grid=(D // block,), out...  8.68 us

profile of v4, /device:TPU:1, one launch (start us, length us, event | category | flops | bytes accessed | tf_op | source)
XLA Modules:
  0.0 121.9 jit_solution(1352204502459860620)
XLA Ops:
  0.6 112.4 %layer.1 = (bf16[8,7168]{1,0:T(8,128)(2,1)}, bf16[8,7168]{1,0:T(8,128)(2,1)}, f32[16,128]{1,0:T(8,128)}, bf16[256,7168]{1,0:T(8,128)(2,1)}, bf16[256,7168]{1,0:T...) custom-call(bf16[8,7168]{1,0:T(8,128)(2,1)} %tok_ref.1, ...), custom_call_target="tpu_custom_call" | custom-call | flops 8000000000 | bytes 20000000 | tf_op jit(solution)/shard_map/layer/pallas_call | solution.py:500
  113.0 8.7 %weight_grads.1 = (bf16[1,7168,256]{2,1,0:T(8,128)(2,1)}, bf16[1,7168,256]{2,1,0:T(8,128)(2,1)}, bf16[1,256,7168]{2,1,0:T(8,128)(2,1)}, bf16[8,7168]{1,0:T(8,128...) custom-call(bf16[256,7168]{1,0:T(8,128)(2,1)} %get-tuple-element.20.x_ref, bf16[256,7168]{1,0:T(8,128)(2,1)} %get-tuple-element.21.g_ref, ...), custom_call_target="tpu_custom_call" | custom-call | flops 3000000000 | bytes 19000000 | tf_op jit(solution)/shard_map/weight_grads/pallas_call | solution.py:546
